TPU v7x, 32 devices: a whole 2x2x4 slice. The times are simulated.
32 devices in a mesh: dp: 8 (over y, x, core), tensor: 4 (over z).
Axes of the slice: x: 2, y: 2, z: 4, core: 2. Of those that a mesh axis runs over, the one named last changes fastest.
Arguments:
- block_input: bfloat16 [8, 1024, 768], P('dp', 'tensor'), may hold values from -6 to 6
- w_q: bfloat16 [768, 768], P('dp', 'tensor'), may hold values from -0.21875 to 0.21875
- w_k: bfloat16 [768, 768], P('dp', 'tensor'), may hold values from -0.21875 to 0.21875
- w_v: bfloat16 [768, 768], P('dp', 'tensor'), may hold values from -0.21875 to 0.21875
- w_o: bfloat16 [768, 768], P('tensor', 'dp'), may hold values from -1.75 to 1.75
- b_q: float32 [768], P('tensor'), may hold values from -3 to 3
- b_v: float32 [768], P('tensor'), may hold values from -3 to 3
- b_o: float32 [768], replicated, may hold values from -2 to 2
- w_1: bfloat16 [768, 3072], P('dp', 'tensor'), may hold values from -0.21875 to 0.21875
- b_1: float32 [3072], P('tensor'), may hold values from -3 to 3
- w_2: bfloat16 [3072, 768], P('tensor', 'dp'), may hold values from -0.109375 to 0.109375
- b_2: float32 [768], replicated, may hold values from -2 to 2
- gain_1: float32 [768], replicated, may hold values from 0.25 to 1.75
- shift_1: float32 [768], replicated, may hold values from -2 to 2
- gain_2: float32 [768], replicated, may hold values from 0.25 to 1.75
- shift_2: float32 [768], replicated, may hold values from -2 to 2
- cotangent: bfloat16 [8, 1024, 768], P('dp', 'tensor'), may hold values from -6 to 6
Outputs:
- block_output: bfloat16 [8, 1024, 768], P('dp', 'tensor')
- grad_x: bfloat16 [8, 1024, 768], P('dp', 'tensor')
- grad_w_q: float32 [768, 768], P('dp', 'tensor')
- grad_w_k: float32 [768, 768], P('dp', 'tensor')
- grad_w_v: float32 [768, 768], P('dp', 'tensor')
- grad_w_o: float32 [768, 768], P('tensor', 'dp')
- grad_b_q: float32 [768], replicated
- grad_b_v: float32 [768], replicated
- grad_b_o: float32 [768], replicated
- grad_w_1: float32 [768, 3072], P('dp', 'tensor')
- grad_b_1: float32 [3072], replicated
- grad_w_2: float32 [3072, 768], P('tensor', 'dp')
- grad_b_2: float32 [768], replicated
- grad_gain_1: float32 [768], replicated
- grad_shift_1: float32 [768], replicated
- grad_gain_2: float32 [768], replicated
- grad_shift_2: float32 [768], replicated
All inputs are finite; a program needn't handle non-finite values.
Results may differ from a plain program's by a relative error of at most 0.019.
Values may be sent and summed in bfloat16 or wider, within the bound.
A program may use at most 128 MiB of HBM per device.

v0:
```python
import jax
import jax.numpy as jnp
from jax import lax
from jax.sharding import PartitionSpec as P

HEAD = 64
QBLK = 512


EPS = 1e-05


def normalize(activity, gain_vec, shift_vec):
    average = jnp.mean(activity, axis=-1, keepdims=True)
    centred = activity - average
    inverse = lax.rsqrt(jnp.mean(centred * centred, axis=-1, keepdims=True) + EPS)
    normed = centred * inverse
    return (normed * gain_vec + shift_vec, normed, inverse)


def normalize_back(upstream, normed, inverse, gain_vec):
    scaled = upstream * gain_vec
    first = jnp.mean(scaled, axis=-1, keepdims=True)
    second = jnp.mean(scaled * normed, axis=-1, keepdims=True)
    grad_in = inverse * (scaled - first - normed * second)
    return (grad_in, jnp.sum(upstream * normed, axis=0), jnp.sum(upstream, axis=0))


def matmul(left_side, right_side):
    return jnp.dot(left_side, right_side, preferred_element_type=jnp.float32)


def contract_rows(left_side, right_side):
    return lax.dot_general(
        left_side, right_side, (((0,), (0,)), ((), ())), preferred_element_type=jnp.float32
    )


def contract_cols(left_side, right_side):
    return lax.dot_general(
        left_side, right_side, (((1,), (1,)), ((), ())), preferred_element_type=jnp.float32
    )


def split_heads(activity):
    return activity.reshape(activity.shape[0], -1, HEAD)


def attend_forward(query_proj, key_proj, value_proj):
    length = query_proj.shape[0]
    score_scale = HEAD ** (-0.5)
    query_heads = split_heads(query_proj)
    key_heads = split_heads(key_proj)
    value_heads = split_heads(value_proj)
    outputs = []
    totals = []
    for number in range(length // QBLK):
        query_block = query_heads[number * QBLK : (number + 1) * QBLK]
        scores = (
            jnp.einsum("qhd,khd->hqk", query_block, key_heads, preferred_element_type=jnp.float32)
            * score_scale
        )
        row_peak = jnp.max(scores, axis=-1, keepdims=True)
        exp_scores = jnp.exp(scores - row_peak)
        row_total = jnp.sum(exp_scores, axis=-1, keepdims=True)
        weights = (exp_scores / row_total).astype(jnp.bfloat16)
        outputs.append(
            jnp.einsum("hqk,khd->qhd", weights, value_heads, preferred_element_type=jnp.float32)
        )
        totals.append(row_peak + jnp.log(row_total))
    mixed_heads = jnp.concatenate(outputs, axis=0).reshape(length, -1).astype(jnp.bfloat16)
    return (mixed_heads, totals)


def attend_backward(query_proj, key_proj, value_proj, grad_mixed, totals):
    length = query_proj.shape[0]
    score_scale = HEAD ** (-0.5)
    query_heads = split_heads(query_proj)
    key_heads = split_heads(key_proj)
    value_heads = split_heads(value_proj)
    grad_heads = split_heads(grad_mixed)
    key_grad = jnp.zeros(key_heads.shape, jnp.float32)
    value_grad = jnp.zeros(value_heads.shape, jnp.float32)
    query_grads = []
    for number in range(length // QBLK):
        query_block = query_heads[number * QBLK : (number + 1) * QBLK]
        grad_block = grad_heads[number * QBLK : (number + 1) * QBLK]
        scores = (
            jnp.einsum("qhd,khd->hqk", query_block, key_heads, preferred_element_type=jnp.float32)
            * score_scale
        )
        probs = jnp.exp(scores - totals[number])
        value_grad = value_grad + jnp.einsum(
            "hqk,qhd->khd",
            probs.astype(jnp.bfloat16),
            grad_block,
            preferred_element_type=jnp.float32,
        )
        grad_probs = jnp.einsum(
            "qhd,khd->hqk", grad_block, value_heads, preferred_element_type=jnp.float32
        )
        inner = jnp.sum(probs * grad_probs, axis=-1, keepdims=True)
        grad_scores = (probs * (grad_probs - inner)).astype(jnp.bfloat16)
        query_grads.append(
            jnp.einsum("hqk,khd->qhd", grad_scores, key_heads, preferred_element_type=jnp.float32)
            * score_scale
        )
        key_grad = (
            key_grad
            + jnp.einsum(
                "hqk,qhd->khd", grad_scores, query_block, preferred_element_type=jnp.float32
            )
            * score_scale
        )
    query_grad = jnp.concatenate(query_grads, axis=0).reshape(length, -1).astype(jnp.bfloat16)
    return (
        query_grad,
        key_grad.reshape(length, -1).astype(jnp.bfloat16),
        value_grad.reshape(length, -1).astype(jnp.bfloat16),
    )


def place_slice(partial_sum, tensor_index, tensor_count):
    width = partial_sum.shape[0]
    empty = jnp.zeros((width * tensor_count,), jnp.float32)
    return lax.dynamic_update_slice(empty, partial_sum, (tensor_index * width,))


def local(
    block_input,
    w_q,
    w_k,
    w_v,
    w_o,
    b_q,
    b_v,
    b_o,
    w_1,
    b_1,
    w_2,
    b_2,
    gain_1,
    shift_1,
    gain_2,
    shift_2,
    cotangent,
):
    tensor_index = lax.axis_index("tensor")
    tensor_count = lax.axis_size("tensor")
    inputs = block_input[0].astype(jnp.float32)
    query_w, key_w, value_w, out_w, up_w, down_w = (
        lax.all_gather(w_q, "dp", axis=0, tiled=True),
        lax.all_gather(w_k, "dp", axis=0, tiled=True),
        lax.all_gather(w_v, "dp", axis=0, tiled=True),
        lax.all_gather(w_o, "dp", axis=1, tiled=True),
        lax.all_gather(w_1, "dp", axis=0, tiled=True),
        lax.all_gather(w_2, "dp", axis=1, tiled=True),
    )
    normed_1, plain_1, inverse_1 = normalize(inputs, gain_1, shift_1)
    full_1 = lax.all_gather(normed_1.astype(jnp.bfloat16), "tensor", axis=0, tiled=True)
    query_proj = (matmul(full_1, query_w) + b_q).astype(jnp.bfloat16)
    key_proj = matmul(full_1, key_w).astype(jnp.bfloat16)
    value_proj = (matmul(full_1, value_w) + b_v).astype(jnp.bfloat16)
    mixed_heads, totals = attend_forward(query_proj, key_proj, value_proj)
    middle = (
        inputs
        + lax.psum_scatter(
            matmul(mixed_heads, out_w).astype(jnp.bfloat16),
            "tensor",
            scatter_dimension=0,
            tiled=True,
        ).astype(jnp.float32)
        + b_o
    )
    normed_2, plain_2, inverse_2 = normalize(middle, gain_2, shift_2)
    full_2 = lax.all_gather(normed_2.astype(jnp.bfloat16), "tensor", axis=0, tiled=True)
    hidden = matmul(full_2, up_w) + b_1
    active = jax.nn.gelu(hidden, approximate=False).astype(jnp.bfloat16)
    result = (
        middle
        + lax.psum_scatter(
            matmul(active, down_w).astype(jnp.bfloat16), "tensor", scatter_dimension=0, tiled=True
        ).astype(jnp.float32)
        + b_2
    )
    upstream = cotangent[0]
    grad_full = lax.all_gather(upstream, "tensor", axis=0, tiled=True)
    grad_active = contract_cols(grad_full, down_w)
    normal_cdf = 0.5 * (1.0 + lax.erf(hidden * 0.7071067811865476))
    normal_pdf = jnp.exp(-0.5 * hidden * hidden) * 0.3989422804014327
    grad_hidden = (grad_active * (normal_cdf + hidden * normal_pdf)).astype(jnp.bfloat16)
    grad_up = contract_rows(full_2, grad_hidden)
    grad_down = contract_rows(active, grad_full)
    bias_one = jnp.sum(grad_hidden.astype(jnp.float32), axis=0)
    grad_norm_2 = lax.psum_scatter(
        contract_cols(grad_hidden, up_w).astype(jnp.bfloat16),
        "tensor",
        scatter_dimension=0,
        tiled=True,
    ).astype(jnp.float32)
    down_in = upstream.astype(jnp.float32)
    grad_mid_norm, gain2_grad, shift2_grad = normalize_back(grad_norm_2, plain_2, inverse_2, gain_2)
    grad_middle = down_in + grad_mid_norm
    bias_two = jnp.sum(down_in, axis=0)
    bias_out = jnp.sum(grad_middle, axis=0)
    grad_mid_full = lax.all_gather(grad_middle.astype(jnp.bfloat16), "tensor", axis=0, tiled=True)
    grad_mixed = contract_cols(grad_mid_full, out_w).astype(jnp.bfloat16)
    grad_out = contract_rows(mixed_heads, grad_mid_full)
    grad_query, grad_key, grad_value = attend_backward(
        query_proj, key_proj, value_proj, grad_mixed, totals
    )
    grad_qw = contract_rows(full_1, grad_query)
    grad_kw = contract_rows(full_1, grad_key)
    grad_vw = contract_rows(full_1, grad_value)
    bias_query = jnp.sum(grad_query.astype(jnp.float32), axis=0)
    bias_value = jnp.sum(grad_value.astype(jnp.float32), axis=0)
    part_q = contract_cols(grad_query, query_w)
    part_k = contract_cols(grad_key, key_w)
    part_v = contract_cols(grad_value, value_w)
    grad_norm_1 = lax.psum_scatter(
        (part_q + part_k + part_v).astype(jnp.bfloat16), "tensor", scatter_dimension=0, tiled=True
    ).astype(jnp.float32)
    grad_in_norm, gain1_grad, shift1_grad = normalize_back(grad_norm_1, plain_1, inverse_1, gain_1)
    grad_input = grad_middle + grad_in_norm
    shard_qw, shard_kw, shard_vw, shard_ow, shard_up, shard_down = (
        lax.psum_scatter(grad_qw, "dp", scatter_dimension=0, tiled=True),
        lax.psum_scatter(grad_kw, "dp", scatter_dimension=0, tiled=True),
        lax.psum_scatter(grad_vw, "dp", scatter_dimension=0, tiled=True),
        lax.psum_scatter(grad_out, "dp", scatter_dimension=1, tiled=True),
        lax.psum_scatter(grad_up, "dp", scatter_dimension=0, tiled=True),
        lax.psum_scatter(grad_down, "dp", scatter_dimension=1, tiled=True),
    )
    small_sums = lax.psum(
        (
            place_slice(bias_query, tensor_index, tensor_count),
            place_slice(bias_value, tensor_index, tensor_count),
            bias_out,
            place_slice(bias_one, tensor_index, tensor_count),
            bias_two,
            gain1_grad,
            shift1_grad,
            gain2_grad,
            shift2_grad,
        ),
        ("dp", "tensor"),
    )
    sum_bq, sum_bv, sum_bo, sum_b1, sum_b2, sum_g1, sum_s1, sum_g2, sum_s2 = small_sums
    return (
        result.astype(jnp.bfloat16)[None],
        grad_input.astype(jnp.bfloat16)[None],
        shard_qw,
        shard_kw,
        shard_vw,
        shard_ow,
        sum_bq,
        sum_bv,
        sum_bo,
        shard_up,
        sum_b1,
        shard_down,
        sum_b2,
        sum_g1,
        sum_s1,
        sum_g2,
        sum_s2,
    )


def solution(mesh):
    in_specs = (
        P("dp", "tensor", None),
        P("dp", "tensor"),
        P("dp", "tensor"),
        P("dp", "tensor"),
        P("tensor", "dp"),
        P("tensor"),
        P("tensor"),
        P(),
        P("dp", "tensor"),
        P("tensor"),
        P("tensor", "dp"),
        P(),
        P(),
        P(),
        P(),
        P(),
        P("dp", "tensor", None),
    )
    out_specs = (
        P("dp", "tensor", None),
        P("dp", "tensor", None),
        P("dp", "tensor"),
        P("dp", "tensor"),
        P("dp", "tensor"),
        P("tensor", "dp"),
        P(),
        P(),
        P(),
        P("dp", "tensor"),
        P(),
        P("tensor", "dp"),
        P(),
        P(),
        P(),
        P(),
        P(),
    )
    return jax.shard_map(local, mesh=mesh, in_specs=in_specs, out_specs=out_specs, check_vma=False)
```

profile of v0, /device:TPU:0, one launch (start us, length us, event | category | flops | bytes accessed | tf_op | source)
XLA Modules:
  0.0 634.0 jit_solution(2741071856451684606)
XLA Ops:
  13.5 11.0 %all_gather.34 = bf16[192,768]{0,1:T(8,128)(2,1)S(1)} all-gather(bf16[192,96]{0,1:T(8,128)(2,1)S(1)} %copy.34), channel_id=1, replica_groups=mesh['dp'=8,'tensor'=4] {'dp'}, dimensions={1}, use_global_device_ids=true | all-gather | bytes 331776 | tf_op jit(solution)/shard_map/all_gather | solution.py:155
  24.5 9.6 %all_gather.32 = bf16[768,192]{1,0:T(8,128)(2,1)S(1)} all-gather(bf16[96,192]{1,0:T(8,128)(2,1)} %param.18), channel_id=1, replica_groups=mesh['dp'=8,'tensor'=4] {'dp'}, dimensions={0}, use_global_device_ids=true | all-gather | bytes 331776 | tf_op jit(solution)/shard_map/all_gather | solution.py:152
  34.1 8.8 %all_gather.33 = bf16[768,192]{1,0:T(8,128)(2,1)S(1)} all-gather(bf16[96,192]{1,0:T(8,128)(2,1)} %param.19), channel_id=1, replica_groups=mesh['dp'=8,'tensor'=4] {'dp'}, dimensions={0}, use_global_device_ids=true | all-gather | bytes 331776 | tf_op jit(solution)/shard_map/all_gather | solution.py:153
  42.9 9.8 %all_gather.31 = bf16[768,192]{1,0:T(8,128)(2,1)S(1)} all-gather(bf16[96,192]{1,0:T(8,128)(2,1)S(1)} %copy-done.31), channel_id=1, replica_groups=mesh['dp'=8,'tensor'=4] {'dp'}, dimensions={0}, use_global_device_ids=true | all-gather | bytes 331776 | tf_op jit(solution)/shard_map/all_gather | solution.py:154
  52.8 2.3 fusion.42
  68.6 35.1 %reduce-scatter.13.cloned.1.call-done = bf16[256,768]{1,0:T(8,128)(2,1)} async-done(((bf16[1024,768]{1,0:T(8,128)(2,1)}), bf16[256,768]{1,0:T(8,128)(2,1)}) %reduce-scatter.13.cloned.1.call-update) | async-done | bytes 393232 | tf_op jit(solution)/shard_map/reduce_scatter | solution.py:167
  109.8 34.4 %all-gather.10.cloned.1.call-done = bf16[1024,768]{1,0:T(8,128)(2,1)} async-done(((bf16[256,768]{1,0:T(8,128)(2,1)}), bf16[1024,768]{1,0:T(8,128)(2,1)}) %all-gather.10.cloned.1.call-update) | async-done | bytes 1572880 | tf_op jit(solution)/shard_map/all_gather | solution.py:176
  144.3 10.6 %fusion.10 = (bf16[1024,768]{1,0:T(8,128)(2,1)}, f32[1024,768]{1,0:T(8,128)}) fusion(f32[768]{0:T(1024)S(1)} %copy-done.49, bf16[1024,768]{1,0:T(8,128)(2,1)} %all-gather.10.cloned.1.call-done, bf16[768,768]{1,0:T(8,128)(2,1)} %all-gather.12.cloned.1.call-done), kind=kOutput, calls=%fused_computation.22 | convolution fusion | flops 1259864064 | bytes 7474176 | tf_op jit(solution)/shard_map/dot_general | solution.py:30
  154.9 13.9 %all-gather.14.cloned.1.call-done = bf16[768,768]{0,1:T(8,128)(2,1)} async-done(((bf16[768,96]{0,1:T(8,128)(2,1)}), bf16[768,768]{0,1:T(8,128)(2,1)}) %all-gather.14.cloned.1.call-update) | async-done | bytes 1179664 | tf_op jit(solution)/shard_map/all_gather | solution.py:157
  168.8 38.5 %all-gather.18.cloned.1.call-done = bf16[1,1024,768]{2,1,0:T(8,128)(2,1)} async-done(((bf16[1,256,768]{2,1,0:T(8,128)(2,1)}), bf16[1,1024,768]{2,1,0:T(8,128)(2,1)}) %all-gather.18.cloned.1.call-update) | async-done | bytes 1572880 | tf_op jit(solution)/shard_map/all_gather | solution.py:187
  207.4 5.5 convert_reduce_fusion
  214.1 2.6 convolution_convert_fusion
  216.8 4.4 convolution_convert_fusion.1
  221.2 29.8 %reduce-scatter.17.cloned.1.call-done = bf16[256,768]{1,0:T(8,128)(2,1)} async-done(((bf16[1024,768]{1,0:T(8,128)(2,1)}), bf16[256,768]{1,0:T(8,128)(2,1)}) %reduce-scatter.17.cloned.1.call-update) | async-done | bytes 393232 | tf_op jit(solution)/shard_map/reduce_scatter | solution.py:195
  253.7 33.8 %reduce-scatter.15.cloned.1.call-done = bf16[256,768]{1,0:T(8,128)(2,1)} async-done(((bf16[1024,768]{1,0:T(8,128)(2,1)}), bf16[256,768]{1,0:T(8,128)(2,1)}) %reduce-scatter.15.cloned.1.call-update) | async-done | bytes 393232 | tf_op jit(solution)/shard_map/reduce_scatter | solution.py:181
  287.4 3.1 fusion.83
  293.1 34.3 %all-gather.16.cloned.1.call-done = bf16[1024,768]{1,0:T(8,128)(2,1)} async-done(((bf16[256,768]{1,0:T(8,128)(2,1)}), bf16[1024,768]{1,0:T(8,128)(2,1)}) %all-gather.16.cloned.1.call-update) | async-done | bytes 1572880 | tf_op jit(solution)/shard_map/all_gather | solution.py:206
  327.4 2.1 convolution_convert_fusion.3
  329.6 4.1 multiply_reduce_fusion.1
  339.2 2.2 fusion.4
  341.4 4.3 multiply_reduce_fusion
  347.6 5.5 multiply_convert_fusion
  361.7 4.8 fusion.93
  366.5 4.8 fusion.30
  375.6 2.5 fusion.90
  378.1 3.3 reduce-scatter.31.cloned.1.call-done
  383.1 35.8 %reduce-scatter.19.cloned.1.call-done = bf16[256,768]{1,0:T(8,128)(2,1)} async-done(((bf16[1024,768]{1,0:T(8,128)(2,1)}), bf16[256,768]{1,0:T(8,128)(2,1)}) %reduce-scatter.19.cloned.1.call-update) | async-done | bytes 393232 | tf_op jit(solution)/shard_map/reduce_scatter | solution.py:220
  420.4 40.5 %all-reduce = (f32[768]{0:T(1024)}, f32[768]{0:T(1024)}, f32[768]{0:T(1024)}, f32[3072]{0:T(1024)}, f32[768]{0:T(1024)}, /*index=5*/f32[768]{0:T(1024)}, f32[768]{0:T(1024)}, f32[768]{0:T(1024)}, f32[768]{0:T(1024)}) all-reduce(f32[768]{0:T(1024)S(1)} %dynamic_update_slice.9, ...), channel_id=1, replica_groups=mesh['dp'=8,'tensor'=4] {'dp','tensor'}, use_global_device_ids=true, to_apply=%region_23.0 | all-reduce | flops 9216 | bytes 73728 | tf_op jit(solution)/shard_map/psum | solution.py:233
  464.0 46.6 %reduce-scatter.29.cloned.1.call-done = f32[768,96]{0,1:T(8,128)} async-done(((f32[768,768]{0,1:T(8,128)}), f32[768,96]{0,1:T(8,128)}) %reduce-scatter.29.cloned.1.call-update) | async-done | bytes 294928 | tf_op jit(solution)/shard_map/reduce_scatter | solution.py:231
  510.6 38.7 %reduce-scatter.25.cloned.1.call-done = f32[96,192]{1,0:T(8,128)} async-done(((f32[768,192]{1,0:T(8,128)}), f32[96,192]{1,0:T(8,128)}) %reduce-scatter.25.cloned.1.call-update) | async-done | bytes 73744 | tf_op jit(solution)/shard_map/reduce_scatter | solution.py:228
  549.3 38.6 %reduce-scatter.23.cloned.1.call-done = f32[96,192]{1,0:T(8,128)} async-done(((f32[768,192]{1,0:T(8,128)}), f32[96,192]{1,0:T(8,128)}) %reduce-scatter.23.cloned.1.call-update) | async-done | bytes 73744 | tf_op jit(solution)/shard_map/reduce_scatter | solution.py:227
  587.9 38.7 %reduce-scatter.21.cloned.1.call-done = f32[96,192]{1,0:T(8,128)} async-done(((f32[768,192]{1,0:T(8,128)}), f32[96,192]{1,0:T(8,128)}) %reduce-scatter.21.cloned.1.call-update) | async-done | bytes 73744 | tf_op jit(solution)/shard_map/reduce_scatter | solution.py:226
  (207 shorter events, 57.5 us)
Async XLA Ops:
  8.0 34.9 %copy-start.31 = (bf16[96,192]{1,0:T(8,128)(2,1)S(1)}, bf16[96,192]{1,0:T(8,128)(2,1)}, u32[]{:S(2)}) copy-start(bf16[96,192]{1,0:T(8,128)(2,1)} %param.20) | copy-start | bytes 110596
  8.0 44.8 %copy-start.46 = (f32[192]{0:T(256)S(1)}, f32[192]{0:T(256)}, u32[]{:S(2)}) copy-start(f32[192]{0:T(256)} %param.22) | copy-start | bytes 2308
  8.0 44.7 %all-gather.8.cloned.1.call-start = ((), (), s32[]{:S(2)}) async-start(), calls=%async_computation.10 | async-start | bytes 1966080 | tf_op jit(solution)/shard_map/all_gather | solution.py:160
  12.5 91.2 %reduce-scatter.13.cloned.1.call-start = ((), (), s32[]{:S(2)}) async-start(), calls=%async_computation.11 | async-start | bytes 1966080 | tf_op jit(solution)/shard_map/reduce_scatter | solution.py:167
  24.5 40.8 %copy-start.11 = (bf16[192,768]{0,1:T(8,128)(2,1)}, bf16[192,768]{0,1:T(8,128)(2,1)S(1)}, u32[]{:S(2)}) copy-start(bf16[192,768]{0,1:T(8,128)(2,1)S(1)} %all_gather.34) | copy-start | bytes 884740
  65.3 38.5 %copy-start.3 = (bf16[1,256,768]{2,1,0:T(8,128)(2,1)S(1)}, bf16[1,256,768]{2,1,0:T(8,128)(2,1)}, u32[]{:S(2)}) copy-start(bf16[1,256,768]{2,1,0:T(8,128)(2,1)} %param.17) | copy-start | bytes 1179652
  65.3 38.5 %copy-start.28 = (f32[768]{0:T(1024)S(1)}, f32[768]{0:T(1024)}, u32[]{:S(2)}) copy-start(f32[768]{0:T(1024)} %param.24) | copy-start | bytes 9220
  65.3 40.9 %copy-start.32 = (f32[768]{0:T(1024)S(1)}, f32[768]{0:T(1024)}, u32[]{:S(2)}) copy-start(f32[768]{0:T(1024)} %param.31) | copy-start | bytes 9220
  65.3 40.9 %copy-start.44 = (f32[768]{0:T(1024)S(1)}, f32[768]{0:T(1024)}, u32[]{:S(2)}) copy-start(f32[768]{0:T(1024)} %param.32) | copy-start | bytes 9220
  68.0 76.3 %copy-start.49 = (f32[768]{0:T(1024)S(1)}, f32[768]{0:T(1024)}, u32[]{:S(2)}) copy-start(f32[768]{0:T(1024)} %param.26) | copy-start | bytes 9220
  68.0 41.8 %all-gather.12.cloned.1.call-start = ((), (), s32[]{:S(2)}) async-start(), calls=%async_computation.13 | async-start | bytes 1327104 | tf_op jit(solution)/shard_map/all_gather | solution.py:156
  68.6 75.7 %all-gather.10.cloned.1.call-start = ((), (), s32[]{:S(2)}) async-start(), calls=%async_computation.12 | async-start | bytes 1966080 | tf_op jit(solution)/shard_map/all_gather | solution.py:176
  108.2 60.6 %all-gather.14.cloned.1.call-start = ((), (), s32[]{:S(2)}) async-start(), calls=%async_computation.14 | async-start | bytes 1327104 | tf_op jit(solution)/shard_map/all_gather | solution.py:157
  108.8 98.5 %all-gather.18.cloned.1.call-start = ((), (), s32[]{:S(2)}) async-start(), calls=%async_computation.24 | async-start | bytes 1966080 | tf_op jit(solution)/shard_map/all_gather | solution.py:187
  109.6 141.4 %reduce-scatter.17.cloned.1.call-start = ((), (), s32[]{:S(2)}) async-start(), calls=%async_computation.16 | async-start | bytes 1966080 | tf_op jit(solution)/shard_map/reduce_scatter | solution.py:195
  216.7 70.7 %reduce-scatter.15.cloned.1.call-start = ((), (), s32[]{:S(2)}) async-start(), calls=%async_computation.15 | async-start | bytes 1966080 | tf_op jit(solution)/shard_map/reduce_scatter | solution.py:181
  216.7 34.2 %copy-start.4 = (bf16[256,768]{1,0:T(8,128)(2,1)S(1)}, bf16[256,768]{1,0:T(8,128)(2,1)}, u32[]{:S(2)}) copy-start(bf16[256,768]{1,0:T(8,128)(2,1)} %reduce-scatter.13.cloned.1.call-done) | copy-start | bytes 1179652
  221.2 106.2 %all-gather.16.cloned.1.call-start = ((), (), s32[]{:S(2)}) async-start(), calls=%async_computation.17 | async-start | bytes 1966080 | tf_op jit(solution)/shard_map/all_gather | solution.py:206
  290.5 39.0 %copy-start.8 = (bf16[1024,192]{0,1:T(8,128)(2,1)S(1)}, bf16[1024,192]{0,1:T(8,128)(2,1)}, u32[]{:S(2)}) copy-start(bf16[1024,192]{0,1:T(8,128)(2,1)} %copy-done.7) | copy-start | bytes 1179652
  291.3 90.1 %reduce-scatter.31.cloned.1.call-start = ((), (), s32[]{:S(2)}) async-start(), calls=%async_computation.25 | async-start | bytes 884736
  347.5 71.4 %reduce-scatter.19.cloned.1.call-start = ((), (), s32[]{:S(2)}) async-start(), calls=%async_computation.18 | async-start | bytes 1966080 | tf_op jit(solution)/shard_map/reduce_scatter | solution.py:220
  361.4 102.7 %reduce-scatter.27.cloned.1.call-start = ((), (), s32[]{:S(2)}) async-start(), calls=%async_computation.22 | async-start | bytes 2654208 | tf_op jit(solution)/shard_map/reduce_scatter | solution.py:230
  366.5 144.2 %reduce-scatter.29.cloned.1.call-start = ((), (), s32[]{:S(2)}) async-start(), calls=%async_computation.23 | async-start | bytes 2654208 | tf_op jit(solution)/shard_map/reduce_scatter | solution.py:231
  371.3 178.0 %reduce-scatter.25.cloned.1.call-start = ((), (), s32[]{:S(2)}) async-start(), calls=%async_computation.21 | async-start | bytes 884736 | tf_op jit(solution)/shard_map/reduce_scatter | solution.py:228
  372.9 214.9 %reduce-scatter.23.cloned.1.call-start = ((), (), s32[]{:S(2)}) async-start(), calls=%async_computation.20 | async-start | bytes 884736 | tf_op jit(solution)/shard_map/reduce_scatter | solution.py:227
  374.5 44.4 %copy-start.33 = (f32[768]{0:T(1024)S(1)}, f32[768]{0:T(1024)}, u32[]{:S(2)}) copy-start(f32[768]{0:T(1024)} %param.29) | copy-start | bytes 9220
  374.5 44.4 %copy-start.38 = (f32[256]{0:T(256)S(1)}, f32[256]{0:T(256)}, u32[]{:S(2)}) copy-start(f32[256]{0:T(256)} %copy-done.37) | copy-start | bytes 3076
  374.5 44.4 %copy-start.40 = (f32[256]{0:T(256)S(1)}, f32[256]{0:T(256)}, u32[]{:S(2)}) copy-start(f32[256]{0:T(256)} %copy-done.39) | copy-start | bytes 3076
  374.5 45.9 %copy-start.41 = (f32[768]{0:T(1024)S(1)}, f32[768]{0:T(1024)}, u32[]{:S(2)}) copy-start(f32[768]{0:T(1024)} %get-tuple-element.17) | copy-start | bytes 9220
  374.5 45.9 %copy-start.42 = (f32[768]{0:T(1024)S(1)}, f32[768]{0:T(1024)}, u32[]{:S(2)}) copy-start(f32[768]{0:T(1024)} %get-tuple-element.23) | copy-start | bytes 9220
  374.5 45.9 %copy-start.43 = (f32[768]{0:T(1024)S(1)}, f32[768]{0:T(1024)}, u32[]{:S(2)}) copy-start(f32[768]{0:T(1024)} %get-tuple-element.34) | copy-start | bytes 9220
  374.6 252.0 %reduce-scatter.21.cloned.1.call-start = ((), (), s32[]{:S(2)}) async-start(), calls=%async_computation.19 | async-start | bytes 884736 | tf_op jit(solution)/shard_map/reduce_scatter | solution.py:226
  (41 other events, 175.6 us)
Sparse Core Ops, SparseCore 0:
  12.7 39.7 all-gather.7
  68.1 35.5 reduce-scatter.12
  216.8 34.1 reduce-scatter.16
  253.1 34.2 reduce-scatter.14
Sparse Core Ops, SparseCore 1:
  70.3 24.1 all-gather.11
  108.3 35.9 all-gather.9
  146.0 22.7 all-gather.13
  170.4 36.9 all-gather.17
  291.4 35.9 all-gather.15
  347.6 33.8 reduce-scatter.30
  383.6 35.2 reduce-scatter.18
  422.7 41.3 reduce-scatter.26
  468.2 42.4 reduce-scatter.28
  514.4 34.9 reduce-scatter.24
  552.9 34.9 reduce-scatter.22
  591.6 34.9 reduce-scatter.20
where the time goes:
time: 638 us; the launch traced here: 634 us
  waiting for transfers between devices  425 us (67%)
  blocking collectives  79.8 us (13%)
  matrix products  73.6 us (12%)
  other arithmetic  30.3 us (5%)
  between operations  16.3 us (3%)
  local copies, waits for them, and re-layouts  8.02 us (1%)
    reduce_scatter x1, waiting for transfers between devices, local(): lax.psum_scatter(grad_down, 'dp', scatter_dimension=1, tiled=True)  46.6 us
    psum x1, blocking collectives, local(): lax.psum((place_slice(bias_query, tensor_index, tensor_count), place_slic...  40.5 us
    reduce_scatter x1, waiting for transfers between devices, local(): lax.psum_scatter(grad_vw, 'dp', scatter_dimension=0, tiled=True)  38.7 us
    reduce_scatter x1, waiting for transfers between devices, local(): lax.psum_scatter(grad_qw, 'dp', scatter_dimension=0, tiled=True)  38.7 us
    reduce_scatter x1, waiting for transfers between devices, local(): lax.psum_scatter(grad_kw, 'dp', scatter_dimension=0, tiled=True)  38.6 us
    all_gather x1, waiting for transfers between devices, local(): grad_full = lax.all_gather(upstream, 'tensor', axis=0, tiled=True)  38.5 us
    reduce_scatter x1, waiting for transfers between devices, local(): lax.psum_scatter((part_q + part_k + part_v).astype(jnp.bfloat16), 'tensor...  35.8 us
    reduce_scatter x1, waiting for transfers between devices, local(): lax.psum_scatter(matmul(mixed_heads, out_w).astype(jnp.bfloat16), 'tensor...  35.1 us
  transfers between devices with their start and end apart: 16, of which 14 were waited for; matrix products, arithmetic and copies ran while one was open for 9% of the time, Pallas kernels for 0%

commit v1 on v0

v1 whole, which is shorter than its diff:
```python
import jax
import jax.numpy as jnp
from jax import lax
from jax.sharding import PartitionSpec as P

HEAD = 64
EPS = 1e-05
BF = jnp.bfloat16
F32 = jnp.float32


def normalize(activity, gain_vec, shift_vec):
    average = jnp.mean(activity, axis=-1, keepdims=True)
    centred = activity - average
    inverse = lax.rsqrt(jnp.mean(centred * centred, axis=-1, keepdims=True) + EPS)
    normed = centred * inverse
    return (normed * gain_vec + shift_vec, normed, inverse)


def normalize_back(upstream, normed, inverse, gain_vec):
    scaled = upstream * gain_vec
    first = jnp.mean(scaled, axis=-1, keepdims=True)
    second = jnp.mean(scaled * normed, axis=-1, keepdims=True)
    grad_in = inverse * (scaled - first - normed * second)
    return (grad_in, jnp.sum(upstream * normed, axis=0), jnp.sum(upstream, axis=0))


def einsum(spec, left_side, right_side):
    return jnp.einsum(spec, left_side, right_side, preferred_element_type=F32)


def split_heads(activity):
    return activity.reshape(activity.shape[0], -1, HEAD)


def attend_forward(query, key, value):
    scale = HEAD ** (-0.5)
    scores = einsum("qhd,khd->hqk", split_heads(query), split_heads(key)) * scale
    peak = jnp.max(scores, axis=-1, keepdims=True)
    exp_scores = jnp.exp(scores - peak)
    total = jnp.sum(exp_scores, axis=-1, keepdims=True)
    weights = (exp_scores / total).astype(BF)
    mixed = einsum("hqk,khd->qhd", weights, split_heads(value))
    return mixed.reshape(query.shape).astype(BF), peak + jnp.log(total)


def attend_backward(query, key, value, grad_mixed, totals):
    scale = HEAD ** (-0.5)
    query_h, key_h, value_h, grad_h = map(split_heads, (query, key, value, grad_mixed))
    probs = jnp.exp(einsum("qhd,khd->hqk", query_h, key_h) * scale - totals)
    grad_value = einsum("hqk,qhd->khd", probs.astype(BF), grad_h)
    grad_probs = einsum("qhd,khd->hqk", grad_h, value_h)
    inner = jnp.sum(probs * grad_probs, axis=-1, keepdims=True)
    grad_scores = (probs * (grad_probs - inner)).astype(BF)
    grad_query = einsum("hqk,khd->qhd", grad_scores, key_h) * scale
    grad_key = einsum("hqk,qhd->khd", grad_scores, query_h) * scale
    return (
        grad_query.reshape(query.shape).astype(BF),
        grad_key.reshape(key.shape).astype(BF),
        grad_value.reshape(key.shape).astype(BF),
    )


ALL = ("tensor", "dp")


def gather_weights(shard, tensor_count):
    full = lax.all_gather(shard, ALL, axis=0, tiled=True)
    return full.reshape(tensor_count, -1, shard.shape[1])


def scatter_weights(full):
    return lax.psum_scatter(
        full.reshape(-1, full.shape[-1]), ALL, scatter_dimension=0, tiled=True
    ).astype(F32)


def local(
    block_input,
    w_q,
    w_k,
    w_v,
    w_o,
    b_q,
    b_v,
    b_o,
    w_1,
    b_1,
    w_2,
    b_2,
    gain_1,
    shift_1,
    gain_2,
    shift_2,
    cotangent,
):
    tensor_count = lax.axis_size("tensor")
    inputs = block_input[0].astype(F32)
    width = inputs.shape[1]
    head_cols = w_q.shape[1]
    normed_1, plain_1, inverse_1 = normalize(inputs, gain_1, shift_1)
    own_1 = normed_1.astype(BF)
    full_1 = lax.all_gather(own_1, "tensor", axis=0, tiled=True)
    packed = gather_weights(jnp.concatenate([w_q, w_k, w_v, w_o.T], axis=1), tensor_count)
    biases = lax.all_gather(jnp.concatenate([b_q, b_v, b_1]), "tensor", axis=0)
    up_w = gather_weights(w_1, tensor_count)
    down_wt = gather_weights(w_2.T, tensor_count)
    packed = packed.reshape(tensor_count, width, 4, head_cols)
    query_w, key_w, value_w, out_wt = packed.transpose(2, 1, 0, 3).reshape(4, width, -1)
    bias_q = biases[:, :head_cols].reshape(-1)
    bias_v = biases[:, head_cols : 2 * head_cols].reshape(-1)
    bias_1 = biases[:, 2 * head_cols :]

    query = (einsum("fd,dc->fc", own_1, query_w) + bias_q).astype(BF)
    key = einsum("fd,dc->fc", full_1, key_w).astype(BF)
    value = (einsum("fd,dc->fc", full_1, value_w) + bias_v).astype(BF)
    mixed, totals = attend_forward(query, key, value)
    middle = inputs + einsum("fc,dc->fd", mixed, out_wt) + b_o
    normed_2, plain_2, inverse_2 = normalize(middle, gain_2, shift_2)
    own_2 = normed_2.astype(BF)
    hidden = einsum("fd,tdc->tfc", own_2, up_w) + bias_1[:, None, :]
    cdf = 0.5 * (1.0 + lax.erf(hidden * 0.7071067811865476))
    active = (hidden * cdf).astype(BF)
    result = middle + einsum("tfc,tdc->fd", active, down_wt) + b_2
    upstream = cotangent[0]
    grad_active = einsum("fd,tdc->tfc", upstream, down_wt)
    pdf = jnp.exp(-0.5 * hidden * hidden) * 0.3989422804014327
    grad_hidden = (grad_active * (cdf + hidden * pdf)).astype(BF)
    grad_up = einsum("fd,tfc->tdc", own_2, grad_hidden).astype(BF)
    grad_down = einsum("fd,tfc->tdc", upstream, active).astype(BF)
    sum_1 = jnp.sum(grad_hidden.astype(F32), axis=1).reshape(-1)
    shard_up = scatter_weights(grad_up)
    shard_down = scatter_weights(grad_down).T
    grad_norm_2 = einsum("tfc,tdc->fd", grad_hidden, up_w)
    down_in = upstream.astype(F32)
    grad_mid_norm, gain2_grad, shift2_grad = normalize_back(grad_norm_2, plain_2, inverse_2, gain_2)
    grad_middle = down_in + grad_mid_norm
    grad_mid = grad_middle.astype(BF)
    grad_mixed = einsum("fd,dc->fc", grad_mid, out_wt).astype(BF)
    grad_query, grad_key, grad_value = attend_backward(query, key, value, grad_mixed, totals)
    part = einsum("fc,dc->fd", grad_key, key_w) + einsum("fc,dc->fd", grad_value, value_w)
    scattered = lax.psum_scatter(part.astype(BF), "tensor", scatter_dimension=0, tiled=True)
    grad_out = einsum("fd,fc->dc", grad_mid, mixed)
    grad_qw = einsum("fd,fc->dc", own_1, grad_query)
    grad_kw = einsum("fd,fc->dc", full_1, grad_key)
    grad_vw = einsum("fd,fc->dc", full_1, grad_value)
    grads = jnp.stack([grad_qw, grad_kw, grad_vw, grad_out]).astype(BF)
    grads = grads.reshape(4, width, tensor_count, head_cols).transpose(2, 1, 0, 3)
    shard = scatter_weights(grads.reshape(tensor_count, width, -1))
    shard_qw, shard_kw, shard_vw, shard_ow = jnp.split(shard, 4, axis=1)
    grad_norm_1 = scattered.astype(F32) + einsum("fc,dc->fd", grad_query, query_w)
    grad_in_norm, gain1_grad, shift1_grad = normalize_back(grad_norm_1, plain_1, inverse_1, gain_1)
    grad_input = grad_middle + grad_in_norm
    pieces = [
        jnp.sum(grad_query.astype(F32), axis=0),
        jnp.sum(grad_value.astype(F32), axis=0),
        jnp.sum(grad_middle, axis=0),
        sum_1,
        jnp.sum(down_in, axis=0),
        gain1_grad,
        shift1_grad,
        gain2_grad,
        shift2_grad,
    ]
    sums = lax.psum(jnp.concatenate(pieces), ALL)
    ends = []
    for piece in pieces:
        ends.append((ends[-1] if ends else 0) + piece.shape[0])
    sum_bq, sum_bv, sum_bo, sum_b1, sum_b2, sum_g1, sum_s1, sum_g2, sum_s2 = jnp.split(
        sums, ends[:-1]
    )
    return (
        result.astype(BF)[None],
        grad_input.astype(BF)[None],
        shard_qw,
        shard_kw,
        shard_vw,
        shard_ow.T,
        sum_bq,
        sum_bv,
        sum_bo,
        shard_up,
        sum_b1,
        shard_down,
        sum_b2,
        sum_g1,
        sum_s1,
        sum_g2,
        sum_s2,
    )


def solution(mesh):
    in_specs = (
        P("dp", "tensor", None),
        P("dp", "tensor"),
        P("dp", "tensor"),
        P("dp", "tensor"),
        P("tensor", "dp"),
        P("tensor"),
        P("tensor"),
        P(),
        P("dp", "tensor"),
        P("tensor"),
        P("tensor", "dp"),
        P(),
        P(),
        P(),
        P(),
        P(),
        P("dp", "tensor", None),
    )
    out_specs = (
        P("dp", "tensor", None),
        P("dp", "tensor", None),
        P("dp", "tensor"),
        P("dp", "tensor"),
        P("dp", "tensor"),
        P("tensor", "dp"),
        P(),
        P(),
        P(),
        P("dp", "tensor"),
        P(),
        P("tensor", "dp"),
        P(),
        P(),
        P(),
        P(),
        P(),
    )
    return jax.shard_map(local, mesh=mesh, in_specs=in_specs, out_specs=out_specs, check_vma=False)
```

time: 638 us -> 681 us (1.067)
  local copies, waits for them, and re-layouts: 8.02 us -> 73.9 us
  blocking collectives: 79.8 us -> 55.9 us
  starting transfers between devices: 1.32 us -> 9.94 us
  waiting for transfers between devices: 425 us -> 417 us
    reduce_scatter x9 -> x3, waiting for transfers between devices: 298 us -> 218 us  [the longest x2 218 us: scatter_weights(): lax.psum_scatter(full.reshape(-1, full.shape[-1]), ALL, scatter_dimension...]
    all_gather x6 -> x4, waiting for transfers between devices: 121 us -> 168 us  [the longest x3 154 us: gather_weights(): full = lax.all_gather(shard, ALL, axis=0, tiled=True)]
    unnamed x116 -> x119, local copies, waits for them, and re-layouts: 7.1 us -> 45.5 us
    unnamed x17 -> x9, waiting for transfers between devices: 5.28 us -> 30.5 us
    all_gather x4 -> x1, blocking collectives: 39.3 us -> 14.8 us  [local(): biases = lax.all_gather(jnp.concatenate([b_q, b_v, b_1]), 'tensor', axis=0)]
    another operation x2 -> x6, local copies, waits for them, and re-layouts: 0.01 us -> 15.6 us  [the longest x1 9.81 us: local(): packed = packed.reshape(tensor_count, width, 4, head_cols)]
    unnamed x1, starting transfers between devices: 0.26 us -> 9.66 us
    dot_general x29 -> x24, matrix products: 71.9 us -> 75.1 us  [einsum(): return jnp.einsum(spec, left_side, right_side, preferred_element_type=F32)]
  transfers between devices with their start and end apart: 16 -> 8, of which waited for: 14 -> 7; matrix products, arithmetic and copies ran while one was open for 9% -> 18% of each run, Pallas kernels for 0% -> 0%
where the time goes in v1:
time: 681 us; the launch traced here: 672 us
  waiting for transfers between devices  417 us (61%)
  matrix products  75.1 us (11%)
  local copies, waits for them, and re-layouts  73.9 us (11%)
  blocking collectives  55.9 us (8%)
  other arithmetic  25.2 us (4%)
  between operations  15 us (2%)
  starting transfers between devices  9.94 us (1%)
    reduce_scatter x2, waiting for transfers between devices, scatter_weights(): lax.psum_scatter(full.reshape(-1, full.shape[-1]), ALL, scatter_dimension...  218 us
    all_gather x3, waiting for transfers between devices, gather_weights(): full = lax.all_gather(shard, ALL, axis=0, tiled=True)  154 us
    dot_general x24, matrix products, einsum(): return jnp.einsum(spec, left_side, right_side, preferred_element_type=F32)  75.1 us
    unnamed x119, local copies, waits for them, and re-layouts  45.5 us
    psum x1, blocking collectives, local(): sums = lax.psum(jnp.concatenate(pieces), ALL)  41.1 us
    unnamed x9, waiting for transfers between devices  30.5 us
    all_gather x1, blocking collectives, local(): biases = lax.all_gather(jnp.concatenate([b_q, b_v, b_1]), 'tensor', axis=0)  14.8 us
    all_gather x1, waiting for transfers between devices, local(): full_1 = lax.all_gather(own_1, 'tensor', axis=0, tiled=True)  14 us
  transfers between devices with their start and end apart: 8, of which 7 were waited for; matrix products, arithmetic and copies ran while one was open for 18% of the time, Pallas kernels for 0%

profile of v1, /device:TPU:0, one launch (start us, length us, event | category | flops | bytes accessed | tf_op | source)
XLA Modules:
  0.0 671.9 jit_solution(4746400948747861600)
XLA Ops:
  12.2 2.0 fusion.54
  16.4 14.8 %all-gather.1 = f32[4,1,1152]{2,1,0:T(1,128)S(1)} all-gather(f32[1,1,1152]{2,1,0:T(1,128)S(1)} %reshape.241), channel_id=2, replica_groups=mesh['dp'=8,'tensor'=4] {'tensor'}, dimensions={0}, use_global_device_ids=true | all-gather | bytes 23040 | tf_op jit(solution)/shard_map/all_gather | solution.py:105
  32.1 45.8 %all-gather.9.cloned.1.call-done = bf16[3072,768]{1,0:T(8,128)(2,1)} async-done(((bf16[96,768]{1,0:T(8,128)(2,1)}), bf16[3072,768]{1,0:T(8,128)(2,1)}) %all-gather.9.cloned.1.call-update) | async-done | bytes 4718608 | tf_op jit(solution)/shard_map/all_gather | solution.py:68
  77.9 6.6 copy.73
  84.5 9.8 %reshape_reshape.6 = bf16[4,768,4,192]{1,0,3,2:T(4,128)(2,1)} reshape(bf16[3072,768]{0,1:T(8,128)(2,1)} %copy.73) | data formatting | bytes 9437184 | tf_op jit(solution)/shard_map/reshape;reshape | solution.py:108
  94.3 3.3 fusion.83
  102.0 14.0 %all-gather.7.cloned.1.call-done = bf16[1024,768]{1,0:T(8,128)(2,1)} async-done(((bf16[256,768]{1,0:T(8,128)(2,1)}), bf16[1024,768]{1,0:T(8,128)(2,1)}) %all-gather.7.cloned.1.call-update) | async-done | bytes 1572880 | tf_op jit(solution)/shard_map/all_gather | solution.py:103
  116.0 3.3 convolution_convert_fusion.2
  122.7 2.7 fusion
  127.2 3.6 fusion.44
  132.3 49.2 %all-gather.11.cloned.1.call-done = bf16[3072,768]{1,0:T(8,128)(2,1)} async-done(((bf16[96,768]{1,0:T(8,128)(2,1)}), bf16[3072,768]{1,0:T(8,128)(2,1)}) %all-gather.11.cloned.1.call-update) | async-done | bytes 4718608 | tf_op jit(solution)/shard_map/all_gather | solution.py:68
  181.4 6.1 fusion.16
  187.6 59.1 %all-gather.13.cloned.1.call-done = bf16[3072,768]{1,0:T(8,128)(2,1)} async-done(((bf16[96,768]{1,0:T(8,128)(2,1)}), bf16[3072,768]{1,0:T(8,128)(2,1)}) %all-gather.13.cloned.1.call-update) | async-done | bytes 4718608 | tf_op jit(solution)/shard_map/all_gather | solution.py:68
  246.7 6.5 convert_reduce_fusion
  253.3 2.2 multiply_reduce_fusion.2
  258.9 7.1 %convert_reduce_fusion.1 = (f32[12,64]{1,0:T(8,128)}, bf16[12,64,1024]{2,1,0:T(8,128)(2,1)S(1)}) fusion(bf16[256,12,64]{0,2,1:T(8,128)(2,1)S(1)} %bitcast.232, f32[12,256,1024]{2,1,0:T(8,128)} %copy-done, f32[12,256]{1,0:T(8,128)S(1)} %log_add_fusion), kind=kOutput, calls=%fused_computation.27 | convolution fusion | flops 414448896 | bytes 14564352 | tf_op jit(solution)/shard_map/hqk,qhd->khd/dot_general | solution.py:29
  266.0 9.6 %multiply_reduce_fusion = (f32[12,256]{1,0:T(8,128)S(1)}, f32[12,256,1024]{2,1,0:T(8,128)}) fusion(f32[12,256,1024]{2,1,0:T(8,128)} %copy-done, f32[12,256]{1,0:T(8,128)S(1)} %log_add_fusion, bf16[256,12,64]{0,2,1:T(8,128)(2,1)S(1)} %bitcast.233, bf16[1024,12,64]{0,2,1:T(8,128)(2,1)S(1)} %bitcast.237), kind=kOutput, calls=%fused_computation.1 | convolution fusion | flops 415233024 | bytes 27156480 | tf_op jit(solution)/shard_map/qhd,khd->hqk/dot_general | solution.py:29
  275.6 6.4 multiply_convert_fusion
  286.5 2.7 add_convert_fusion
  289.2 9.7 %reduce-scatter.13.cloned.1.call-start = ((), (), s32[]{:S(2)}) async-start(), calls=%async_computation.11 | async-start | bytes 4866048
  299.0 5.0 convert_reduce_fusion.4
  308.9 2.5 maximum_bitcast_fusion
  311.4 10.2 %copy.92 = bf16[4,768,4,192]{3,2,1,0:T(4,128)(2,1)} copy(bf16[4,768,4,192]{1,3,0,2:T(8,128)(2,1)} %maximum_bitcast_fusion) | data formatting | bytes 9437184
  321.7 11.6 %reshape.253 = bf16[3072,768]{1,0:T(8,128)(2,1)} reshape(bf16[4,768,4,192]{3,2,1,0:T(4,128)(2,1)} %copy.92) | data formatting | bytes 9437184
  334.7 4.4 convolution_convert_fusion.1
  340.5 4.6 convolution_convert_fusion
  352.5 5.3 fusion.45
  357.9 2.3 fusion.60
  365.4 41.1 %psum.7 = f32[9216]{0:T(1024)S(1)} all-reduce(f32[9216]{0:T(1024)} %constant_dynamic-update-slice_fusion), channel_id=1, replica_groups=mesh['dp'=8,'tensor'=4] {'tensor','dp'}, use_global_device_ids=true, to_apply=%region_22.0 | all-reduce | flops 9216 | bytes 73728 | tf_op jit(solution)/shard_map/psum | solution.py:165
  410.1 29.1 %reduce-scatter.13.cloned.1.call-done = bf16[96,768]{1,0:T(8,128)(2,1)} async-done(((bf16[3072,768]{1,0:T(8,128)(2,1)}), bf16[96,768]{1,0:T(8,128)(2,1)}) %reduce-scatter.13.cloned.1.call-update) | async-done | bytes 147472
  442.6 109.1 %reduce-scatter.9.cloned.1.call-done = bf16[96,768]{1,0:T(8,128)(2,1)} async-done(((bf16[3072,768]{1,0:T(8,128)(2,1)}), bf16[96,768]{1,0:T(8,128)(2,1)}) %reduce-scatter.9.cloned.1.call-update) | async-done | bytes 147472 | tf_op jit(solution)/shard_map/reduce_scatter | solution.py:73
  554.0 109.3 %reduce-scatter.11.cloned.1.call-done = bf16[96,768]{1,0:T(8,128)(2,1)} async-done(((bf16[3072,768]{1,0:T(8,128)(2,1)}), bf16[96,768]{1,0:T(8,128)(2,1)}) %reduce-scatter.11.cloned.1.call-update) | async-done | bytes 147472 | tf_op jit(solution)/shard_map/reduce_scatter | solution.py:73
  (182 shorter events, 57.8 us)
Async XLA Ops:
  7.2 70.7 %all-gather.9.cloned.1.call-start = ((), (), s32[]{:S(2)}) async-start(), calls=%async_computation.5 | async-start | bytes 4866048 | tf_op jit(solution)/shard_map/all_gather | solution.py:68
  9.8 106.2 %all-gather.7.cloned.1.call-start = ((), (), s32[]{:S(2)}) async-start(), calls=%async_computation.4 | async-start | bytes 1966080 | tf_op jit(solution)/shard_map/all_gather | solution.py:103
  11.0 88.1 %copy-start.28 = (f32[256]{0:T(256)}, f32[256]{0:T(256)S(1)}, u32[]{:S(2)}) copy-start(f32[256]{0:T(256)S(1)} %broadcast_multiply_fusion.5) | copy-start | bytes 3076
  12.2 86.9 %copy-start.33 = (f32[256]{0:T(256)}, f32[256]{0:T(256)S(1)}, u32[]{:S(2)}) copy-start(f32[256]{0:T(256)S(1)} %add_rsqrt_fusion.1) | copy-start | bytes 3076
  14.3 167.2 %all-gather.11.cloned.1.call-start = ((), (), s32[]{:S(2)}) async-start(), calls=%async_computation.6 | async-start | bytes 4866048 | tf_op jit(solution)/shard_map/all_gather | solution.py:68
  15.0 231.7 %all-gather.13.cloned.1.call-start = ((), (), s32[]{:S(2)}) async-start(), calls=%async_computation.7 | async-start | bytes 4866048 | tf_op jit(solution)/shard_map/all_gather | solution.py:68
  15.6 342.2 %reduce-scatter.7.cloned.1.call-start = ((), (), s32[]{:S(2)}) async-start(), calls=%async_computation.8 | async-start | bytes 1966080 | tf_op jit(solution)/shard_map/reduce_scatter | solution.py:142
  130.8 56.7 %copy-start.11 = (bf16[12,64,256]{2,1,0:T(8,128)(2,1)}, bf16[12,64,256]{2,1,0:T(8,128)(2,1)S(1)}, u32[]{:S(2)}) copy-start(bf16[12,64,256]{2,1,0:T(8,128)(2,1)S(1)} %fusion.44) | copy-start | bytes 1179652
  131.4 50.0 %copy-start.36 = (f32[256]{0:T(256)}, f32[256]{0:T(256)S(1)}, u32[]{:S(2)}) copy-start(f32[256]{0:T(256)S(1)} %broadcast_multiply_fusion.4) | copy-start | bytes 3076
  181.4 65.2 %copy-start.16 = (bf16[1,256,768]{2,1,0:T(8,128)(2,1)S(1)}, bf16[1,256,768]{2,1,0:T(8,128)(2,1)}, u32[]{:S(2)}) copy-start(bf16[1,256,768]{2,1,0:T(8,128)(2,1)} %param.33) | copy-start | bytes 1179652
  246.7 6.5 copy-start.32
  246.7 6.5 copy-start.37
  246.7 6.5 copy-start.41
  246.7 6.5 copy-start.45
  258.8 7.1 %copy-start.10 = (bf16[1024,768]{0,1:T(8,128)(2,1)S(1)}, bf16[1024,768]{0,1:T(8,128)(2,1)}, u32[]{:S(2)}) copy-start(bf16[1024,768]{0,1:T(8,128)(2,1)} %copy-done.9) | copy-start | bytes 4718596
  258.8 16.8 %slice-start = ((s8[12582912]{0:T(1024)(128)(4,1)}), s8[4194304]{0:T(1024)(128)(4,1)S(1)}, s32[]{:S(2)}) async-start(s8[12582912]{0:T(1024)(128)(4,1)} %bitcast.219), calls=%async_computation.12 | async-start | bytes 8388608
  258.8 16.8 %slice-start.1 = ((s8[12582912]{0:T(1024)(128)(4,1)}), s8[4194304]{0:T(1024)(128)(4,1)S(1)}, s32[]{:S(2)}) async-start(s8[12582912]{0:T(1024)(128)(4,1)} %bitcast.219), calls=%async_computation.13 | async-start | bytes 8388608
  266.0 20.2 %copy-start.18 = (bf16[12,64,1024]{2,1,0:T(8,128)(2,1)}, bf16[12,64,1024]{2,1,0:T(8,128)(2,1)S(1)}, u32[]{:S(2)}) copy-start(bf16[12,64,1024]{2,1,0:T(8,128)(2,1)S(1)} %get-tuple-element.126) | copy-start | bytes 4718596
  266.0 9.6 %slice-start.2 = ((s8[12582912]{0:T(1024)(128)(4,1)}), s8[4194304]{0:T(1024)(128)(4,1)S(1)}, s32[]{:S(2)}) async-start(s8[12582912]{0:T(1024)(128)(4,1)} %bitcast.219), calls=%async_computation.14 | async-start | bytes 8388608
  286.5 12.4 %copy-start.4 = (bf16[1024,768]{0,1:T(8,128)(2,1)S(1)}, bf16[1024,768]{0,1:T(8,128)(2,1)}, u32[]{:S(2)}) copy-start(bf16[1024,768]{0,1:T(8,128)(2,1)} %copy-done.3) | copy-start | bytes 4718596
  289.2 14.8 %copy-start.26 = (f32[768]{0:T(1024)S(1)}, f32[768]{0:T(1024)}, u32[]{:S(2)}) copy-start(f32[768]{0:T(1024)} %param.29) | copy-start | bytes 9220
  289.2 14.8 %copy-start.29 = (f32[256]{0:T(256)S(1)}, f32[256]{0:T(256)}, u32[]{:S(2)}) copy-start(f32[256]{0:T(256)} %copy-done.28) | copy-start | bytes 3076
  289.2 150.0 %reduce-scatter.13.cloned.1.call-start = ((), (), s32[]{:S(2)}) async-start(), calls=%async_computation.11 | async-start | bytes 4866048
  298.9 5.1 copy-start.31
  298.9 5.7 copy-start.12
  333.3 218.4 %reduce-scatter.9.cloned.1.call-start = ((), (), s32[]{:S(2)}) async-start(), calls=%async_computation.9 | async-start | bytes 4866048 | tf_op jit(solution)/shard_map/reduce_scatter | solution.py:73
  339.1 324.2 %reduce-scatter.11.cloned.1.call-start = ((), (), s32[]{:S(2)}) async-start(), calls=%async_computation.10 | async-start | bytes 4866048 | tf_op jit(solution)/shard_map/reduce_scatter | solution.py:73
  345.2 6.1 copy-start.38
  352.5 5.3 copy-start.8
  352.5 5.3 copy-start.21
  352.5 5.3 copy-start.35
  357.8 6.3 copy-start.43
  (27 other events, 68.8 us)
Sparse Core Ops, SparseCore 0:
  11.5 66.3 all-gather.8
  80.0 35.8 all-gather.6
  118.9 62.4 all-gather.10
  184.2 62.4 all-gather.12
  289.3 34.0 reduce-scatter.6
  333.4 105.8 reduce-scatter.12
  445.6 106.0 reduce-scatter.8
  557.2 106.0 reduce-scatter.10
